TPU v7x, 256 devices: a whole 4x4x8 slice. The times are simulated.
256 devices in a mesh: row: 32 (over x, z_lo, core), col: 8 (over y, z_hi).
Axes of the slice: x: 4, y: 4, z: 8 (z_hi: 2, z_lo: 4; z = z_hi * 4 + z_lo), core: 2. Of those that a mesh axis runs over, the one named last changes fastest.
Arguments:
- tokens: bfloat16 [512, 8192], P('col', 'row'), may hold values from -6 to 6
- gate_weight: bfloat16 [8192, 28672], P('row', 'col'), may hold values from -0.0625 to 0.0625
- up_weight: bfloat16 [8192, 28672], P('row', 'col'), may hold values from -0.0625 to 0.0625
- down_weight: bfloat16 [28672, 8192], P('col', 'row'), may hold values from -0.03125 to 0.03125
- out_grad: bfloat16 [512, 8192], P('col', 'row'), may hold values from -6 to 6
Outputs:
- layer_out: bfloat16 [512, 8192], P('col', 'row')
- token_grad: bfloat16 [512, 8192], P('col', 'row')
- gate_grad: bfloat16 [8192, 28672], P('row', 'col')
- up_grad: bfloat16 [8192, 28672], P('row', 'col')
- down_grad: bfloat16 [28672, 8192], P('col', 'row')
All inputs are finite; a program needn't handle non-finite values.
Results may differ from a plain program's by a relative error of at most 0.0067.
Values may be sent and summed in bfloat16 or wider, within the bound.
A program may use at most 128 MiB of HBM per device.

v0:
```python
import jax
import jax.numpy as jnp
from jax import lax
from jax.sharding import PartitionSpec as P


def activate(gate, up):
    gate_value = gate.astype(jnp.float32)
    return (gate_value * jax.nn.sigmoid(gate_value) * up.astype(jnp.float32)).astype(jnp.bfloat16)


def deltas(hidden_grad, gate, up):
    gate_value = gate.astype(jnp.float32)
    up_value = up.astype(jnp.float32)
    sigma = jax.nn.sigmoid(gate_value)
    gate_delta = (hidden_grad * up_value * sigma * (1.0 + gate_value * (1.0 - sigma))).astype(
        jnp.bfloat16
    )
    up_delta = (hidden_grad * gate_value * sigma).astype(jnp.bfloat16)
    return (gate_delta, up_delta)


def contract_last(left, right):
    return lax.dot_general(
        left, right, (((1,), (1,)), ((), ())), preferred_element_type=jnp.float32
    )


def contract_first(left, right):
    return lax.dot_general(
        left, right, (((0,), (0,)), ((), ())), preferred_element_type=jnp.float32
    )


def local(tokens, gate_weight, up_weight, down_weight, out_grad):
    hidden_width = gate_weight.shape[1]
    token_full = lax.all_gather(tokens, "col", axis=0, tiled=True)
    both_weight = jnp.concatenate((gate_weight, up_weight), axis=1)
    summed = lax.psum_scatter(
        jnp.dot(token_full, both_weight, preferred_element_type=jnp.float32),
        "row",
        scatter_dimension=0,
        tiled=True,
    )
    gate_part = summed[:, :hidden_width].astype(jnp.bfloat16)
    up_part = summed[:, hidden_width:].astype(jnp.bfloat16)
    hidden_part = activate(gate_part, up_part)
    hidden_full = lax.all_gather(hidden_part, "row", axis=0, tiled=True)
    layer_out = lax.psum_scatter(
        jnp.dot(hidden_full, down_weight, preferred_element_type=jnp.float32),
        "col",
        scatter_dimension=0,
        tiled=True,
    ).astype(jnp.bfloat16)
    cotan_full = lax.all_gather(out_grad, "col", axis=0, tiled=True)
    down_grad = contract_first(hidden_full, cotan_full).astype(jnp.bfloat16)
    hidden_grad = lax.psum_scatter(
        contract_last(cotan_full, down_weight), "row", scatter_dimension=0, tiled=True
    )
    gate_local, up_local = deltas(hidden_grad, gate_part, up_part)
    gate_delta, up_delta = (
        lax.all_gather(gate_local, "row", axis=0, tiled=True),
        lax.all_gather(up_local, "row", axis=0, tiled=True),
    )
    token_grad = lax.psum_scatter(
        contract_last(gate_delta, gate_weight) + contract_last(up_delta, up_weight),
        "col",
        scatter_dimension=0,
        tiled=True,
    ).astype(jnp.bfloat16)
    gate_grad = contract_first(token_full, gate_delta).astype(jnp.bfloat16)
    up_grad = contract_first(token_full, up_delta).astype(jnp.bfloat16)
    return (layer_out, token_grad, gate_grad, up_grad, down_grad)


def solution(mesh):
    placed = (P("col", "row"), P("row", "col"), P("row", "col"), P("col", "row"), P("col", "row"))
    return jax.shard_map(
        local,
        mesh=mesh,
        in_specs=placed,
        out_specs=(
            P("col", "row"),
            P("col", "row"),
            P("row", "col"),
            P("row", "col"),
            P("col", "row"),
        ),
        check_vma=False,
    )
```

profile of v0, /device:TPU:2, one launch (start us, length us, event | category | flops | bytes accessed | tf_op | source)
XLA Modules:
  0.0 791.7 jit_solution(3175294987909523581)
XLA Ops:
  7.2 0.0 copy-start
  7.2 0.0 reduce-scatter.13.cloned.1.call-start
  7.2 46.5 %all_gather.15 = bf16[512,256]{1,0:T(8,128)(2,1)S(1)} all-gather(bf16[64,256]{1,0:T(8,128)(2,1)} %param.5), channel_id=1, replica_groups=mesh['row'=32,'col'=8] {'col'}, dimensions={0}, use_global_device_ids=true | all-gather | bytes 294912 | tf_op jit(solution)/shard_map/all_gather | solution.py:37
  53.7 9.3 %convolution_bitcast_fusion = f32[512,7168]{0,1:T(8,128)} fusion(bf16[512,256]{1,0:T(8,128)(2,1)S(1)} %all_gather.15, bf16[256,3584]{1,0:T(8,128)(2,1)} %param.7, bf16[256,3584]{1,0:T(8,128)(2,1)} %param.6), kind=kOutput, calls=%fused_computation | convolution fusion | flops 1886388224 | bytes 18612224 | tf_op jit(solution)/shard_map/dot_general | solution.py:40
  63.1 14.4 %copy.26 = f32[512,7168]{1,0:T(8,128)} copy(f32[512,7168]{0,1:T(8,128)} %convolution_bitcast_fusion) | data formatting | bytes 29360128
  77.5 0.0 copy-start.1
  77.5 0.0 reduce-scatter.13.cloned.1.call-update
  77.5 0.0 reduce-scatter.15.cloned.1.call-start
  77.5 0.7 copy-done.1
  78.2 46.4 %all_gather.17 = bf16[512,256]{1,0:T(8,128)(2,1)S(1)} all-gather(bf16[64,256]{1,0:T(8,128)(2,1)S(1)} %copy-done.1), channel_id=1, replica_groups=mesh['row'=32,'col'=8] {'col'}, dimensions={0}, use_global_device_ids=true | all-gather | bytes 294912 | tf_op jit(solution)/shard_map/all_gather | solution.py:55
  124.6 0.0 copy-done
  124.6 4.1 fusion.17
  128.7 0.0 reduce-scatter.15.cloned.1.call-update
  128.7 0.0 all-gather.6.cloned.1.call-start
  128.8 125.9 %reduce-scatter.13.cloned.1.call-done = f32[16,7168]{1,0:T(8,128)} async-done(((f32[512,7168]{1,0:T(8,128)}), f32[16,7168]{1,0:T(8,128)}) %reduce-scatter.13.cloned.1.call-update) | async-done | bytes 458768 | tf_op jit(solution)/shard_map/reduce_scatter | solution.py:39
  254.7 1.0 convert.4
  255.7 147.9 %reduce-scatter.15.cloned.1.call-done = f32[16,3584]{1,0:T(8,128)} async-done(((f32[512,3584]{1,0:T(8,128)}), f32[16,3584]{1,0:T(8,128)}) %reduce-scatter.15.cloned.1.call-update) | async-done | bytes 229392 | tf_op jit(solution)/shard_map/reduce_scatter | solution.py:57
  403.6 1.8 fusion.14
  405.4 0.0 all-gather.6.cloned.1.call-update
  405.4 0.0 all-gather.8.cloned.1.call-start
  405.4 0.5 all-gather.8.cloned.1.call-update
  406.0 0.0 all-gather.4.cloned.1.call-start
  406.0 0.5 all-gather.4.cloned.1.call-update
  406.6 0.0 reduce-scatter.11.cloned.1.call-start
  406.6 77.2 %all-gather.6.cloned.1.call-done = bf16[512,3584]{1,0:T(8,128)(2,1)} async-done(((bf16[16,3584]{1,0:T(8,128)(2,1)}), bf16[512,3584]{1,0:T(8,128)(2,1)}) %all-gather.6.cloned.1.call-update) | async-done | bytes 3670032 | tf_op jit(solution)/shard_map/all_gather | solution.py:62
  483.8 3.8 fusion.18
  487.6 59.8 %all-gather.8.cloned.1.call-done = bf16[512,3584]{1,0:T(8,128)(2,1)} async-done(((bf16[16,3584]{1,0:T(8,128)(2,1)}), bf16[512,3584]{1,0:T(8,128)(2,1)}) %all-gather.8.cloned.1.call-update) | async-done | bytes 3670032 | tf_op jit(solution)/shard_map/all_gather | solution.py:63
  547.4 4.5 convolution_add_fusion
  551.9 0.0 reduce-scatter.11.cloned.1.call-update
  551.9 0.0 reduce-scatter.9.cloned.1.call-start
  552.0 58.9 %all-gather.4.cloned.1.call-done = bf16[512,3584]{1,0:T(8,128)(2,1)} async-done(((bf16[16,3584]{1,0:T(8,128)(2,1)}), bf16[512,3584]{1,0:T(8,128)(2,1)}) %all-gather.4.cloned.1.call-update) | async-done | bytes 3670032 | tf_op jit(solution)/shard_map/all_gather | solution.py:48
  610.9 3.9 fusion.16
  614.9 0.0 reduce-scatter.9.cloned.1.call-update
  614.9 4.4 fusion
  619.3 3.8 copy.23
  623.1 4.4 fusion.1
  627.6 3.8 copy.24
  631.4 4.4 convolution_convert_fusion
  635.8 62.7 %reduce-scatter.11.cloned.1.call-done = f32[64,256]{1,0:T(8,128)} async-done(((f32[512,256]{1,0:T(8,128)}), f32[64,256]{1,0:T(8,128)}) %reduce-scatter.11.cloned.1.call-update) | async-done | bytes 65552 | tf_op jit(solution)/shard_map/reduce_scatter | solution.py:65
  698.5 1.5 convert_element_type.46
  700.0 83.4 %reduce-scatter.9.cloned.1.call-done = f32[64,256]{1,0:T(8,128)} async-done(((f32[512,256]{1,0:T(8,128)}), f32[64,256]{1,0:T(8,128)}) %reduce-scatter.9.cloned.1.call-update) | async-done | bytes 65552 | tf_op jit(solution)/shard_map/reduce_scatter | solution.py:49
  783.4 1.5 convert_element_type.43
Async XLA Ops:
  7.2 117.5 %copy-start = (bf16[3584,256]{1,0:T(8,128)(2,1)S(1)}, bf16[3584,256]{1,0:T(8,128)(2,1)}, u32[]{:S(2)}) copy-start(bf16[3584,256]{1,0:T(8,128)(2,1)} %param.8) | copy-start | bytes 5505028
  7.2 247.5 %reduce-scatter.13.cloned.1.call-start = ((), (), s32[]{:S(2)}) async-start(), calls=%async_computation.9 | async-start | bytes 15138816 | tf_op jit(solution)/shard_map/reduce_scatter | solution.py:39
  77.5 0.8 copy-start.1
  77.5 326.1 %reduce-scatter.15.cloned.1.call-start = ((), (), s32[]{:S(2)}) async-start(), calls=%async_computation.10 | async-start | bytes 7569408 | tf_op jit(solution)/shard_map/reduce_scatter | solution.py:57
  128.7 355.1 %all-gather.6.cloned.1.call-start = ((), (), s32[]{:S(2)}) async-start(), calls=%async_computation.6 | async-start | bytes 3784704 | tf_op jit(solution)/shard_map/all_gather | solution.py:62
  405.4 142.0 %all-gather.8.cloned.1.call-start = ((), (), s32[]{:S(2)}) async-start(), calls=%async_computation.7 | async-start | bytes 3784704 | tf_op jit(solution)/shard_map/all_gather | solution.py:63
  406.0 204.9 %all-gather.4.cloned.1.call-start = ((), (), s32[]{:S(2)}) async-start(), calls=%async_computation.4 | async-start | bytes 3784704 | tf_op jit(solution)/shard_map/all_gather | solution.py:48
  406.6 292.0 %reduce-scatter.11.cloned.1.call-start = ((), (), s32[]{:S(2)}) async-start(), calls=%async_computation.8 | async-start | bytes 589824 | tf_op jit(solution)/shard_map/reduce_scatter | solution.py:65
  551.9 231.4 %reduce-scatter.9.cloned.1.call-start = ((), (), s32[]{:S(2)}) async-start(), calls=%async_computation.5 | async-start | bytes 589824 | tf_op jit(solution)/shard_map/reduce_scatter | solution.py:49
Sparse Core Ops, SparseCore 0:
  77.6 177.0 reduce-scatter.12
  257.2 146.3 reduce-scatter.14
  406.0 77.7 all-gather.5
  486.1 61.2 all-gather.7
  549.7 61.2 all-gather.3
  614.6 83.8 reduce-scatter.10
  702.9 80.4 reduce-scatter.8
where the time goes:
time: 792 us
  waiting for transfers between devices  617 us (78%)
  blocking collectives  92.9 us (12%)
  matrix products  39 us (5%)
  local copies, waits for them, and re-layouts  22.7 us (3%)
  between operations  14.2 us (2%)
    reduce_scatter x1, waiting for transfers between devices, local(): lax.psum_scatter(contract_last(cotan_full, down_weight), 'row', scatter_d...  148 us
    reduce_scatter x1, waiting for transfers between devices, local(): lax.psum_scatter(jnp.dot(token_full, both_weight, preferred_element_type=...  126 us
    reduce_scatter x1, waiting for transfers between devices, local(): lax.psum_scatter(jnp.dot(hidden_full, down_weight, preferred_element_type...  83.4 us
    all_gather x1, waiting for transfers between devices, local(): lax.all_gather(gate_local, 'row', axis=0, tiled=True)  77.2 us
    reduce_scatter x1, waiting for transfers between devices, local(): lax.psum_scatter(contract_last(gate_delta, gate_weight) + contract_last(u...  62.7 us
    all_gather x1, waiting for transfers between devices, local(): lax.all_gather(up_local, 'row', axis=0, tiled=True)  59.8 us
    all_gather x1, waiting for transfers between devices, local(): hidden_full = lax.all_gather(hidden_part, 'row', axis=0, tiled=True)  58.9 us
    all_gather x1, blocking collectives, local(): token_full = lax.all_gather(tokens, 'col', axis=0, tiled=True)  46.5 us
  transfers between devices with their start and end apart: 7, of which 7 were waited for; matrix products, arithmetic and copies ran while one was open for 5% of the time, Pallas kernels for 0%

commit v1 on v0

v1 whole, which is shorter than its diff:
```python
import jax
import jax.numpy as jnp
from jax import lax
from jax.experimental import pallas as pl
from jax.experimental.pallas import tpu as pltpu
from jax.sharding import PartitionSpec as P

MESH = pl.DeviceIdType.MESH
BF = jnp.bfloat16
F32 = jnp.float32
NP = 7
W = 256
HALF = NP * W
F = 256


def dot(a, b, dims):
    return lax.dot_general(a, b, (dims, ((), ())), preferred_element_type=F32)


NN = ((1,), (0,))
NT = ((1,), (1,))
TN = ((0,), (0,))


def kernel(
    tok, gate_w, up_w, down_w, cot,
    lo_ref, tg_ref, gate_g, up_g, down_g,
    tc, wgu, wd, s32, sb, r1, a2, r2, yb, zr, ag, go, do, acc, e1b, e2b, e2r, e3b, e3r,
    in_l, wl, ws, wr, zh_s, zh_r, y_s, y_r, co_s, co_r,
    x_s, x_r, z_s, z_r, za_s, za_r, xa_s, xa_r, ol, os_, or_,
    e1_s, e1_r, e2_s, e2_r, e3_s, e3_r,
):
    row, col = lax.axis_index("row"), lax.axis_index("col")
    x, zl, c = row // 8, (row // 2) % 4, row % 2
    y, zh = col // 2, col % 2
    xp, xm, x2 = (x + 1) % 4, (x + 3) % 4, (x + 2) % 4

    def at_x(px):
        return (px * 8 + zl * 2 + c, col)

    def z_of(dz):
        b = (zl % 2) if dz % 2 == 0 else 1 - zl % 2
        h = (zl // 2) if dz < 2 else 1 - zl // 2
        return h * 2 + b

    def at_z(dz):
        return (x * 8 + z_of(dz) * 2 + c, col)

    def at_y(dy):
        return (row, ((y + dy) % 4) * 2 + zh)

    at_co = (x * 8 + zl * 2 + 1 - c, col)
    at_zh = (row, y * 2 + 1 - zh)
    peers = [at_co, at_zh, at_x(xp), at_x(xm)]
    peers += [at_z(d) for d in (1, 2, 3)] + [at_y(d) for d in (1, 2, 3)]

    def remote(src, dst, ss, rs, dev):
        return pltpu.make_async_remote_copy(
            src_ref=src, dst_ref=dst, send_sem=ss, recv_sem=rs, device_id=dev, device_id_type=MESH
        )

    def cols(core, k):
        return pl.ds(pl.multiple_of(core * HALF + k * W, W), W)

    def feats(core):
        return pl.ds(pl.multiple_of(core * F, F), F)

    def rows(start, size):
        return pl.ds(pl.multiple_of(start, size), size)

    def w_local(k):
        return (
            pltpu.make_async_copy(gate_w.at[:, cols(c, k)], wgu.at[k, feats(c), pl.ds(0, W)], wl.at[k, 0]),
            pltpu.make_async_copy(up_w.at[:, cols(c, k)], wgu.at[k, feats(c), pl.ds(W, W)], wl.at[k, 1]),
            pltpu.make_async_copy(down_w.at[cols(c, k), :], wd.at[k, :, feats(c)], wl.at[k, 2]),
        )

    def w_remote(k):
        o = 1 - c
        return (
            remote(gate_w.at[:, cols(o, k)], wgu.at[k, feats(c), pl.ds(0, W)], ws.at[k, 0], wr.at[k, 0], at_co),
            remote(up_w.at[:, cols(o, k)], wgu.at[k, feats(c), pl.ds(W, W)], ws.at[k, 1], wr.at[k, 1], at_co),
            remote(down_w.at[cols(o, k), :], wd.at[k, :, feats(c)], ws.at[k, 2], wr.at[k, 2], at_co),
        )

    def block(j):
        return tc.at[:, rows(j * 64, 64), feats(c)]

    def b_zh():
        return remote(block(col), block(col), zh_s, zh_r, at_zh)

    def b_y(h, dy):
        b = block(y * 2 + (zh if h == 0 else 1 - zh))
        return remote(b, b, y_s.at[h, dy - 1], y_r.at[h, dy - 1], at_y(dy))

    def b_co(j):
        return remote(block(j), block(j), co_s.at[j], co_r.at[j], at_co)

    ins = (
        pltpu.make_async_copy(tok, tc.at[0, rows(col * 64, 64), feats(c)], in_l.at[0]),
        pltpu.make_async_copy(cot, tc.at[1, rows(col * 64, 64), feats(c)], in_l.at[1]),
    )
    for d in ins:
        d.start()

    @pl.loop(0, NP)
    def _(k):
        for d in w_local(k):
            d.start()

    barrier = pltpu.get_barrier_semaphore()
    for p in peers:
        pl.semaphore_signal(barrier, inc=1, device_id=p, device_id_type=MESH)
    pl.semaphore_wait(barrier, len(peers))

    for d in ins:
        d.wait()
    b_zh().start()
    for dy in (1, 2, 3):
        b_y(0, dy).start()
    b_co(col).start()

    @pl.loop(0, NP)
    def _(k):
        for d in w_remote(k):
            d.start()

    acc[...] = jnp.zeros_like(acc)
    b_zh().wait_recv()
    for dy in (1, 2, 3):
        b_y(1, dy).start()
    b_co(y * 2 + 1 - zh).start()
    for h in (0, 1):
        for dy in (1, 2, 3):
            b_y(h, dy).wait_recv()
            b_co(((y + 4 - dy) % 4) * 2 + (zh if h == 0 else 1 - zh)).start()

    @pl.loop(0, 8)
    def _(j):
        b_co(j).wait_recv()

    def chunk(px):
        return pl.multiple_of(px * 128, 128)

    def x_copy(k, i):
        if i == 0:
            src, dst, to = sb.at[k, rows(chunk(x2), 64)], r1.at[k, 0], xp
        elif i == 1:
            src, dst, to = sb.at[k, rows(chunk(x2) + 64, 64)], r1.at[k, 1], xm
        elif i == 2:
            src, dst, to = sb.at[k, rows(chunk(xp) + 64, 64)], r2.at[k, 0, pl.ds(64, 64)], xp
        elif i == 3:
            src, dst, to = sb.at[k, rows(chunk(xm), 64)], r2.at[k, 1, pl.ds(0, 64)], xm
        elif i == 4:
            src, dst, to = a2.at[k, 0], r2.at[k, 0, pl.ds(0, 64)], xp
        else:
            src, dst, to = a2.at[k, 1], r2.at[k, 1, pl.ds(64, 64)], xm
        return remote(src, dst, x_s.at[k, i], x_r.at[k, i], at_x(to))

    def z_copy(k, dz):
        src = yb.at[k, rows(z_of(dz) * 32, 32)]
        return remote(src, zr.at[k, dz - 1], z_s.at[k, dz - 1], z_r.at[k, dz - 1], at_z(dz))

    def za_copy(k, dz):
        mine = ag.at[k, rows(x * 128 + zl * 32, 32)]
        return remote(mine, mine, za_s.at[k, dz - 1], za_r.at[k, dz - 1], at_z(dz))

    def xa_copy(k, i):
        if i < 2:
            part, to = ag.at[k, rows(chunk(x), 128)], (xp, xm)[i]
        elif i == 2:
            part, to = ag.at[k, rows(chunk(xm), 64)], xp
        else:
            part, to = ag.at[k, rows(chunk(xp) + 64, 64)], xm
        return remote(part, part, xa_s.at[k, i], xa_r.at[k, i], at_x(to))

    def out_local(k):
        return (
            pltpu.make_async_copy(go.at[k, feats(c), pl.ds(0, W)], gate_g.at[:, cols(c, k)], ol.at[k, 0]),
            pltpu.make_async_copy(go.at[k, feats(c), pl.ds(W, W)], up_g.at[:, cols(c, k)], ol.at[k, 1]),
            pltpu.make_async_copy(do.at[k, :, feats(c)], down_g.at[cols(c, k), :], ol.at[k, 2]),
        )

    def out_remote(k):
        o = 1 - c
        return (
            remote(go.at[k, feats(o), pl.ds(0, W)], gate_g.at[:, cols(c, k)], os_.at[k, 0], or_.at[k, 0], at_co),
            remote(go.at[k, feats(o), pl.ds(W, W)], up_g.at[:, cols(c, k)], os_.at[k, 1], or_.at[k, 1], at_co),
            remote(do.at[k, :, feats(o)], down_g.at[cols(c, k), :], os_.at[k, 2], or_.at[k, 2], at_co),
        )

    def s0(k):
        for d in w_local(k):
            d.wait()
        for d in w_remote(k):
            d.wait_recv()
        b = k % 4
        p = dot(tc[0], wgu[k], NN)
        s32[b, :, : 2 * W] = p
        sb[k, :, : 2 * W] = p.astype(BF)
        q = dot(tc[1], wd[k], NT)
        s32[b, :, 2 * W :] = q
        sb[k, :, 2 * W :] = q.astype(BF)
        for i in range(4):
            x_copy(k, i).start()

    def s1(k):
        b = k % 4
        x_copy(k, 0).wait_recv()
        a2[k, 0] = (s32[b, rows(chunk(xp), 64)] + r1[k, 0].astype(F32)).astype(BF)
        x_copy(k, 4).start()
        x_copy(k, 1).wait_recv()
        a2[k, 1] = (s32[b, rows(chunk(xm) + 64, 64)] + r1[k, 1].astype(F32)).astype(BF)
        x_copy(k, 5).start()

    def s2(k):
        b = k % 4
        for i in (2, 3, 4, 5):
            x_copy(k, i).wait_recv()
        total = s32[b, rows(chunk(x), 128)] + (r2[k, 0].astype(F32) + r2[k, 1].astype(F32))
        s32[b, rows(chunk(x), 128)] = total
        yb[k] = total.astype(BF)
        for dz in (2, 1, 3):
            z_copy(k, dz).start()

    def s3(k):
        b = k % 4
        for dz in (1, 2, 3):
            z_copy(k, dz).wait_recv()
        total = s32[b, rows(chunk(x) + zl * 32, 32)]
        for i in range(3):
            total = total + zr[k, i].astype(F32)
        g = total[:, :W]
        u = total[:, W : 2 * W]
        hg = total[:, 2 * W :]
        s = 1.0 / (1.0 + jnp.exp(-g))
        here = rows(x * 128 + zl * 32, 32)
        ag[k, here, :W] = (hg * u * s * (1.0 + g * (1.0 - s))).astype(BF)
        ag[k, here, W : 2 * W] = (hg * g * s).astype(BF)
        ag[k, here, 2 * W :] = (g * s * u).astype(BF)
        for dz in (2, 1, 3):
            za_copy(k, dz).start()

    def s4(k):
        for dz in (1, 2, 3):
            za_copy(k, dz).wait_recv()
        xa_copy(k, 0).start()
        xa_copy(k, 1).start()

    def s5(k):
        xa_copy(k, 0).wait_recv()
        xa_copy(k, 2).start()
        xa_copy(k, 1).wait_recv()
        xa_copy(k, 3).start()

    def s6(k):
        xa_copy(k, 2).wait_recv()
        xa_copy(k, 3).wait_recv()
        go[k] = dot(tc[0], ag[k, :, : 2 * W], TN).astype(BF)
        do[k] = dot(ag[k, :, 2 * W :], tc[1], TN).astype(BF)
        for d in out_remote(k):
            d.start()
        for d in out_local(k):
            d.start()
        acc[1] += dot(ag[k, :, : 2 * W], wgu[k], NT)
        acc[0] += dot(ag[k, :, 2 * W :], wd[k], NN)

    @pl.loop(0, NP + 6)
    def _(t):
        for lag, stage in ((0, s0), (1, s1), (2, s2), (3, s3), (4, s4), (5, s5), (6, s6)):
            k = t - lag

            @pl.when((k >= 0) & (k < NP))
            def _(k=k, stage=stage):
                stage(k)

    def e1(i):
        return remote(acc.at[i, :, feats(1 - c)], e1b.at[i], e1_s.at[i], e1_r.at[i], at_co)

    def e2(dy):
        src = e2b.at[:, rows(((y + dy) % 4) * 128, 128)]
        return remote(src, e2r.at[dy - 1], e2_s.at[dy - 1], e2_r.at[dy - 1], at_y(dy))

    def e3():
        return remote(e3b, e3r, e3_s, e3_r, at_zh)

    for i in (0, 1):
        e1(i).start()
    for i in (0, 1):
        e1(i).wait_recv()
        total = acc[i, :, feats(c)] + e1b[i]
        e1b[i] = total
        e2b[i] = total.astype(BF)
    for dy in (2, 1, 3):
        e2(dy).start()
    for dy in (1, 2, 3):
        e2(dy).wait_recv()
    there, mine = rows(y * 128 + (1 - zh) * 64, 64), rows(y * 128 + zh * 64, 64)
    rt, rm = rows((1 - zh) * 64, 64), rows(zh * 64, 64)
    away = e1b[:, there]
    for i in range(3):
        away = away + e2r[i, :, rt].astype(F32)
    e3b[...] = away.astype(BF)
    e3().start()
    kept = e1b[:, mine]
    for i in range(3):
        kept = kept + e2r[i, :, rm].astype(F32)
    e3().wait_recv()
    kept = (kept + e3r[...].astype(F32)).astype(BF)
    lo_ref[...] = kept[0]
    tg_ref[...] = kept[1]

    b_zh().wait_send()
    for h in (0, 1):
        for dy in (1, 2, 3):
            b_y(h, dy).wait_send()

    @pl.loop(0, 8)
    def _(j):
        b_co(j).wait_send()

    @pl.loop(0, NP)
    def _(k):
        for d in w_remote(k):
            d.wait_send()
        for i in range(6):
            x_copy(k, i).wait_send()
        for dz in (1, 2, 3):
            z_copy(k, dz).wait_send()
            za_copy(k, dz).wait_send()
        for i in range(4):
            xa_copy(k, i).wait_send()
        for d in out_local(k):
            d.wait()
        for d in out_remote(k):
            d.wait()

    for i in (0, 1):
        e1(i).wait_send()
    for dy in (1, 2, 3):
        e2(dy).wait_send()
    e3().wait_send()


def local(tokens, gate_weight, up_weight, down_weight, out_grad):
    def v(*shape, t=BF):
        return pltpu.VMEM(shape, t)

    def sem(*shape):
        return pltpu.SemaphoreType.DMA(shape) if shape else pltpu.SemaphoreType.DMA

    W3 = 3 * W
    anywhere = pl.BlockSpec(memory_space=pl.ANY)
    vmem = pl.BlockSpec(memory_space=pltpu.VMEM)
    macs = 9 * 512 * 256 * 3584
    return pl.pallas_call(
        kernel,
        out_shape=(
            jax.ShapeDtypeStruct((64, 256), BF),
            jax.ShapeDtypeStruct((64, 256), BF),
            jax.ShapeDtypeStruct((256, 3584), BF),
            jax.ShapeDtypeStruct((256, 3584), BF),
            jax.ShapeDtypeStruct((3584, 256), BF),
        ),
        in_specs=[anywhere] * 5,
        out_specs=(vmem, vmem, anywhere, anywhere, anywhere),
        scratch_shapes=[
            v(2, 512, 512),
            v(NP, 512, 2 * W),
            v(NP, W, 512),
            v(4, 512, W3, t=F32),
            v(NP, 512, W3),
            v(NP, 2, 64, W3),
            v(NP, 2, 64, W3),
            v(NP, 2, 128, W3),
            v(NP, 128, W3),
            v(NP, 3, 32, W3),
            v(NP, 512, W3),
            v(NP, 512, 2 * W),
            v(NP, W, 512),
            v(2, 512, 512, t=F32),
            v(2, 512, 256, t=F32),
            v(2, 512, 256),
            v(3, 2, 128, 256),
            v(2, 64, 256),
            v(2, 64, 256),
            sem(2), sem(NP, 3), sem(NP, 3), sem(NP, 3),
            sem(), sem(), sem(2, 3), sem(2, 3), sem(8), sem(8),
            sem(NP, 6), sem(NP, 6), sem(NP, 3), sem(NP, 3),
            sem(NP, 3), sem(NP, 3), sem(NP, 4), sem(NP, 4),
            sem(NP, 3), sem(NP, 3), sem(NP, 3),
            sem(2), sem(2), sem(3), sem(3), sem(), sem(),
        ],
        compiler_params=pltpu.CompilerParams(
            collective_id=0, has_side_effects=True, vmem_limit_bytes=60 * 2**20
        ),
        cost_estimate=pl.CostEstimate(flops=2 * macs, bytes_accessed=12 * 2**20, transcendentals=2**16),
        name="swiglu",
    )(tokens, gate_weight, up_weight, down_weight, out_grad)


def solution(mesh):
    tokens, weights = P("col", "row"), P("row", "col")
    return jax.shard_map(
        local,
        mesh=mesh,
        in_specs=(tokens, weights, weights, tokens, tokens),
        out_specs=(tokens, tokens, weights, weights, tokens),
        check_vma=False,
    )
```

time: 792 us -> 146 us (0.18)
  waiting for transfers between devices: 617 us -> 0 us
  Pallas kernels: 0 us -> 135 us
  blocking collectives: 92.9 us -> 0 us
  matrix products: 39 us -> 0 us
  local copies, waits for them, and re-layouts: 22.7 us -> 9.12 us
  between operations: 14.2 us -> 0.64 us
    reduce_scatter x4 -> x0, waiting for transfers between devices: 420 us -> none  [the longest x1 148 us: local(): lax.psum_scatter(contract_last(cotan_full, down_weight), 'row', scatter_d...]
    all_gather x3 -> x0, waiting for transfers between devices: 196 us -> none  [the longest x1 77.2 us: local(): lax.all_gather(gate_local, 'row', axis=0, tiled=True)]
    pallas_call x0 -> x1, Pallas kernels: none -> 135 us  [local(): pl.pallas_call(kernel, out_shape=(jax.ShapeDtypeStruct((64, 256), BF), ja...]
    all_gather x2 -> x0, blocking collectives: 92.9 us -> none  [the longest x1 46.5 us: local(): token_full = lax.all_gather(tokens, 'col', axis=0, tiled=True)]
    dot_general x7 -> x0, matrix products: 34.9 us -> none  [the longest x3 13.3 us: contract_first(): lax.dot_general(left, right, (((0,), (0,)), ((), ())), preferred_element_...]
    unnamed x7 -> x9, local copies, waits for them, and re-layouts: 22.7 us -> 9.12 us
  transfers between devices with their start and end apart: 7 -> 0, of which waited for: 7 -> 0; matrix products, arithmetic and copies ran while one was open for 5% -> 0% of each run, Pallas kernels for 0% -> 0%
where the time goes in v1:
time: 146 us; the launch traced here: 145 us
  Pallas kernels  135 us (92%)
  local copies, waits for them, and re-layouts  9.12 us (6%)
    pallas_call x1, Pallas kernels, local(): pl.pallas_call(kernel, out_shape=(jax.ShapeDtypeStruct((64, 256), BF), ja...  135 us
    unnamed x9, local copies, waits for them, and re-layouts  9.12 us

profile of v1, /device:TPU:2, one launch (start us, length us, event | category | flops | bytes accessed | tf_op | source)
XLA Modules:
  0.0 144.5 jit_solution(3284398877164507251)
XLA Ops:
  0.6 134.8 %swiglu.1 = (bf16[64,256]{1,0:T(8,128)(2,1)}, bf16[64,256]{1,0:T(8,128)(2,1)}, bf16[256,3584]{1,0:T(8,128)(2,1)}, bf16[256,3584]{1,0:T(8,128)(2,1)}, bf16[3584,256]{1,0:T(8,128)(2,1)}) custom-call(bf16[64,256]{1,0:T(8,128)(2,1)} %tok.1, bf16[256,3584]{1,0:T(8,128)(2,1)} %gate_w.1, bf16[256,3584]{1,0:T(8,128)(2,1)} %up_w.1, bf16[3584,256]{1,0:T(8,128)(2,1)} %down_w.1, ...), custom_call_target="tpu_custom_call" | custom-call | flops 8455716864 | bytes 12582912 | tf_op jit(solution)/shard_map/swiglu/pallas_call | solution.py:357
  135.4 1.4 copy.15
  136.8 1.4 copy.16
  138.1 0.0 copy-start.1
  138.2 3.0 %copy.17 = bf16[256,3584]{1,0:T(8,128)(2,1)} copy(bf16[256,3584]{1,0:T(8,128)(2,1)} %get-tuple-element.12) | data formatting | bytes 3670016
  141.1 0.0 copy-done.1
  141.1 0.0 copy-start
  141.1 1.2 copy.18
  142.4 0.9 copy-done
  143.3 1.2 copy.19
Async XLA Ops:
  138.1 3.0 %copy-start.1 = (bf16[256,3584]{1,0:T(8,128)(2,1)S(1)}, bf16[256,3584]{1,0:T(8,128)(2,1)}, u32[]{:S(2)}) copy-start(bf16[256,3584]{1,0:T(8,128)(2,1)} %get-tuple-element.13) | copy-start | bytes 5505028
  141.1 2.2 %copy-start = (bf16[3584,256]{1,0:T(8,128)(2,1)S(1)}, bf16[3584,256]{1,0:T(8,128)(2,1)}, u32[]{:S(2)}) copy-start(bf16[3584,256]{1,0:T(8,128)(2,1)} %get-tuple-element.14) | copy-start | bytes 5505028

commit v2 on v1

--- a/solution.py
+++ b/solution.py
@@ -10,6 +10,7 @@
 F32 = jnp.float32
 NP = 7
 W = 256
+AHEAD = 2
 HALF = NP * W
 F = 256
 
@@ -26,9 +27,10 @@
 def kernel(
     tok, gate_w, up_w, down_w, cot,
     lo_ref, tg_ref, gate_g, up_g, down_g,
-    tc, wgu, wd, s32, sb, r1, a2, r2, yb, zr, ag, go, do, acc, e1b, e2b, e2r, e3b, e3r,
+    tc, wgu, wd, s32, sb, r1, a2, r2, yb, zr,
+    h32, hs, hz1, hb, hr1, ha, hr2, hy, hz2, ag, hg, go, do, acc, e1b, e2b, e2r, e3b, e3r,
     in_l, wl, ws, wr, zh_s, zh_r, y_s, y_r, co_s, co_r,
-    x_s, x_r, z_s, z_r, za_s, za_r, xa_s, xa_r, ol, os_, or_,
+    x_s, x_r, z_s, z_r, za_s, za_r, xa_s, xa_r, h_s, h_r, ha_s, ha_r, ol, os_, or_,
     e1_s, e1_r, e2_s, e2_r, e3_s, e3_r,
 ):
     row, col = lax.axis_index("row"), lax.axis_index("col")
@@ -103,15 +105,15 @@
     )
     for d in ins:
         d.start()
+    barrier = pltpu.get_barrier_semaphore()
+    for p in peers:
+        pl.semaphore_signal(barrier, inc=1, device_id=p, device_id_type=MESH)
 
     @pl.loop(0, NP)
     def _(k):
         for d in w_local(k):
             d.start()
 
-    barrier = pltpu.get_barrier_semaphore()
-    for p in peers:
-        pl.semaphore_signal(barrier, inc=1, device_id=p, device_id_type=MESH)
     pl.semaphore_wait(barrier, len(peers))
 
     for d in ins:
@@ -120,9 +122,7 @@
     for dy in (1, 2, 3):
         b_y(0, dy).start()
     b_co(col).start()
-
-    @pl.loop(0, NP)
-    def _(k):
+    for k in range(AHEAD):
         for d in w_remote(k):
             d.start()
 
@@ -139,6 +139,8 @@
     @pl.loop(0, 8)
     def _(j):
         b_co(j).wait_recv()
+
+    b0, b1 = zl % 2, zl // 2
 
     def chunk(px):
         return pl.multiple_of(px * 128, 128)
@@ -162,6 +164,27 @@
         src = yb.at[k, rows(z_of(dz) * 32, 32)]
         return remote(src, zr.at[k, dz - 1], z_s.at[k, dz - 1], z_r.at[k, dz - 1], at_z(dz))
 
+    def h_copy(k, i):
+        to = xp if i in (1, 3, 5) else xm
+        if i == 0:
+            src, dst = hs.at[k, :, :, 1 - b0], hz1.at[k]
+        elif i == 1:
+            src, dst = hb.at[k, x2, 0], hr1.at[k, 0]
+        elif i == 2:
+            src, dst = hb.at[k, x2, 1], hr1.at[k, 1]
+        elif i == 3:
+            src, dst = hb.at[k, xp, 1], hr2.at[k, 0, 1]
+        elif i == 4:
+            src, dst = hb.at[k, xm, 0], hr2.at[k, 1, 0]
+        elif i == 5:
+            src, dst = ha.at[k, 0], hr2.at[k, 0, 0]
+        elif i == 6:
+            src, dst = ha.at[k, 1], hr2.at[k, 1, 1]
+        else:
+            src, dst = hy.at[k], hz2.at[k]
+        dev = at_z(1) if i == 0 else at_z(2) if i == 7 else at_x(to)
+        return remote(src, dst, h_s.at[k, i], h_r.at[k, i], dev)
+
     def za_copy(k, dz):
         mine = ag.at[k, rows(x * 128 + zl * 32, 32)]
         return remote(mine, mine, za_s.at[k, dz - 1], za_r.at[k, dz - 1], at_z(dz))
@@ -175,6 +198,21 @@
             part, to = ag.at[k, rows(chunk(xp) + 64, 64)], xm
         return remote(part, part, xa_s.at[k, i], xa_r.at[k, i], at_x(to))
 
+    def ha_copy(k, i):
+        if i == 0:
+            part, dev = hg.at[k, x, b1, b0], at_z(2)
+        elif i == 1:
+            part, dev = hg.at[k, x, :, b0], at_x(xp)
+        elif i == 2:
+            part, dev = hg.at[k, x, :, b0], at_x(xm)
+        elif i == 3:
+            part, dev = hg.at[k, xm, 0, b0], at_x(xp)
+        elif i == 4:
+            part, dev = hg.at[k, xp, 1, b0], at_x(xm)
+        else:
+            part, dev = hg.at[k, :, :, b0], at_z(1)
+        return remote(part, part, ha_s.at[k, i], ha_r.at[k, i], dev)
+
     def out_local(k):
         return (
             pltpu.make_async_copy(go.at[k, feats(c), pl.ds(0, W)], gate_g.at[:, cols(c, k)], ol.at[k, 0]),
@@ -195,27 +233,34 @@
             d.wait()
         for d in w_remote(k):
             d.wait_recv()
-        b = k % 4
+        b = k % 5
         p = dot(tc[0], wgu[k], NN)
-        s32[b, :, : 2 * W] = p
-        sb[k, :, : 2 * W] = p.astype(BF)
-        q = dot(tc[1], wd[k], NT)
-        s32[b, :, 2 * W :] = q
-        sb[k, :, 2 * W :] = q.astype(BF)
+        s32[b] = p
+        sb[k] = p.astype(BF)
         for i in range(4):
             x_copy(k, i).start()
+        q = dot(tc[1], wd[k], NT).reshape(4, 2, 2, 32, W)
+        h32[b] = q
+        hs[k] = q.astype(BF)
+        h_copy(k, 0).start()
 
     def s1(k):
-        b = k % 4
+        b = k % 5
         x_copy(k, 0).wait_recv()
         a2[k, 0] = (s32[b, rows(chunk(xp), 64)] + r1[k, 0].astype(F32)).astype(BF)
         x_copy(k, 4).start()
         x_copy(k, 1).wait_recv()
         a2[k, 1] = (s32[b, rows(chunk(xm) + 64, 64)] + r1[k, 1].astype(F32)).astype(BF)
         x_copy(k, 5).start()
+        h_copy(k, 0).wait_recv()
+        half = h32[b, :, :, b0] + hz1[k].astype(F32)
+        h32[b, :, :, b0] = half
+        hb[k] = half.astype(BF)
+        for i in (1, 2, 3, 4):
+            h_copy(k, i).start()
 
     def s2(k):
-        b = k % 4
+        b = k % 5
         for i in (2, 3, 4, 5):
             x_copy(k, i).wait_recv()
         total = s32[b, rows(chunk(x), 128)] + (r2[k, 0].astype(F32) + r2[k, 1].astype(F32))
@@ -223,77 +268,147 @@
         yb[k] = total.astype(BF)
         for dz in (2, 1, 3):
             z_copy(k, dz).start()
+        h_copy(k, 1).wait_recv()
+        ha[k, 0] = (h32[b, xp, 0, b0] + hr1[k, 0].astype(F32)).astype(BF)
+        h_copy(k, 5).start()
+        h_copy(k, 2).wait_recv()
+        ha[k, 1] = (h32[b, xm, 1, b0] + hr1[k, 1].astype(F32)).astype(BF)
+        h_copy(k, 6).start()
 
     def s3(k):
-        b = k % 4
+        b = k % 5
+        for i in (3, 4, 5, 6):
+            h_copy(k, i).wait_recv()
+        total = h32[b, x, :, b0] + (hr2[k, 0].astype(F32) + hr2[k, 1].astype(F32))
+        h32[b, x, :, b0] = total
+        hy[k] = h32[b, x, 1 - b1, b0].astype(BF)
+        h_copy(k, 7).start()
+
+    def s4(k):
+        b = k % 5
         for dz in (1, 2, 3):
             z_copy(k, dz).wait_recv()
         total = s32[b, rows(chunk(x) + zl * 32, 32)]
         for i in range(3):
             total = total + zr[k, i].astype(F32)
-        g = total[:, :W]
-        u = total[:, W : 2 * W]
-        hg = total[:, 2 * W :]
+        g, u = total[:, :W], total[:, W:]
         s = 1.0 / (1.0 + jnp.exp(-g))
+        hg[k, x, b1, b0] = (g * s * u).astype(BF)
+        ha_copy(k, 0).start()
+        h_copy(k, 7).wait_recv()
+        grad = h32[b, x, b1, b0] + hz2[k].astype(F32)
         here = rows(x * 128 + zl * 32, 32)
-        ag[k, here, :W] = (hg * u * s * (1.0 + g * (1.0 - s))).astype(BF)
-        ag[k, here, W : 2 * W] = (hg * g * s).astype(BF)
-        ag[k, here, 2 * W :] = (g * s * u).astype(BF)
+        ag[k, here, :W] = (grad * u * s * (1.0 + g * (1.0 - s))).astype(BF)
+        ag[k, here, W:] = (grad * g * s).astype(BF)
         for dz in (2, 1, 3):
             za_copy(k, dz).start()
 
-    def s4(k):
+    def s5(k):
+        ha_copy(k, 0).wait_recv()
+        ha_copy(k, 1).start()
+        ha_copy(k, 2).start()
         for dz in (1, 2, 3):
             za_copy(k, dz).wait_recv()
         xa_copy(k, 0).start()
         xa_copy(k, 1).start()
 
-    def s5(k):
+    def s6(k):
+        ha_copy(k, 1).wait_recv()
+        ha_copy(k, 3).start()
+        ha_copy(k, 2).wait_recv()
+        ha_copy(k, 4).start()
         xa_copy(k, 0).wait_recv()
         xa_copy(k, 2).start()
         xa_copy(k, 1).wait_recv()
         xa_copy(k, 3).start()
 
-    def s6(k):
+    def s7(k):
+        ha_copy(k, 3).wait_recv()
+        ha_copy(k, 4).wait_recv()
+        ha_copy(k, 5).start()
         xa_copy(k, 2).wait_recv()
         xa_copy(k, 3).wait_recv()
-        go[k] = dot(tc[0], ag[k, :, : 2 * W], TN).astype(BF)
-        do[k] = dot(ag[k, :, 2 * W :], tc[1], TN).astype(BF)
-        for d in out_remote(k):
+        go[k] = dot(tc[0], ag[k], TN).astype(BF)
+        for d in out_remote(k)[:2]:
             d.start()
-        for d in out_local(k):
+        for d in out_local(k)[:2]:
             d.start()
-        acc[1] += dot(ag[k, :, : 2 * W], wgu[k], NT)
-        acc[0] += dot(ag[k, :, 2 * W :], wd[k], NN)
-
-    @pl.loop(0, NP + 6)
+        acc[1] += dot(ag[k], wgu[k], NT)
+
+    def s8(k):
+        ha_copy(k, 5).wait_recv()
+        h = hg[k].reshape(512, W)
+        do[k] = dot(h, tc[1], TN).astype(BF)
+        out_remote(k)[2].start()
+        out_local(k)[2].start()
+        acc[0] += dot(h, wd[k], NN)
+
+    @pl.loop(0, NP + 8)
     def _(t):
-        for lag, stage in ((0, s0), (1, s1), (2, s2), (3, s3), (4, s4), (5, s5), (6, s6)):
+        @pl.when(t < NP - AHEAD)
+        def _():
+            for d in w_remote(t + AHEAD):
+                d.start()
+
+        for lag, stage in enumerate((s0, s1, s2, s3, s4, s5, s6, s7, s8)):
             k = t - lag
 
             @pl.when((k >= 0) & (k < NP))
             def _(k=k, stage=stage):
                 stage(k)
 
-    def e1(i):
-        return remote(acc.at[i, :, feats(1 - c)], e1b.at[i], e1_s.at[i], e1_r.at[i], at_co)
+    def part(dy):
+        return rows(((y + dy) % 4) * 128, 128)
+
+    def e1(dy):
+        src, dst = acc.at[:, part(dy), feats(1 - c)], e1b.at[:, part(dy)]
+        return remote(src, dst, e1_s.at[dy], e1_r.at[dy], at_co)
 
     def e2(dy):
-        src = e2b.at[:, rows(((y + dy) % 4) * 128, 128)]
+        src = e2b.at[:, part(dy)]
         return remote(src, e2r.at[dy - 1], e2_s.at[dy - 1], e2_r.at[dy - 1], at_y(dy))
 
     def e3():
         return remote(e3b, e3r, e3_s, e3_r, at_zh)
 
-    for i in (0, 1):
-        e1(i).start()
-    for i in (0, 1):
-        e1(i).wait_recv()
-        total = acc[i, :, feats(c)] + e1b[i]
-        e1b[i] = total
-        e2b[i] = total.astype(BF)
+    for dy in (2, 1, 3, 0):
+        e1(dy).start()
     for dy in (2, 1, 3):
+        e1(dy).wait_recv()
+        e2b[:, part(dy)] = (acc[:, part(dy), feats(c)] + e1b[:, part(dy)]).astype(BF)
         e2(dy).start()
+    e1(0).wait_recv()
+    e1b[:, part(0)] = acc[:, part(0), feats(c)] + e1b[:, part(0)]
+
+    b_zh().wait_send()
+    for h in (0, 1):
+        for dy in (1, 2, 3):
+            b_y(h, dy).wait_send()
+
+    @pl.loop(0, 8)
+    def _(j):
+        b_co(j).wait_send()
+
+    @pl.loop(0, NP)
+    def _(k):
+        for d in w_remote(k):
+            d.wait_send()
+        for i in range(6):
+            x_copy(k, i).wait_send()
+        for dz in (1, 2, 3):
+            z_copy(k, dz).wait_send()
+            za_copy(k, dz).wait_send()
+        for i in range(4):
+            xa_copy(k, i).wait_send()
+        for i in range(8):
+            h_copy(k, i).wait_send()
+        for i in range(6):
+            ha_copy(k, i).wait_send()
+        for d in out_local(k):
+            d.wait()
+        for d in out_remote(k):
+            d.wait()
+
     for dy in (1, 2, 3):
         e2(dy).wait_recv()
     there, mine = rows(y * 128 + (1 - zh) * 64, 64), rows(y * 128 + zh * 64, 64)
@@ -311,38 +426,36 @@
     lo_ref[...] = kept[0]
     tg_ref[...] = kept[1]
 
-    b_zh().wait_send()
-    for h in (0, 1):
-        for dy in (1, 2, 3):
-            b_y(h, dy).wait_send()
-
-    @pl.loop(0, 8)
-    def _(j):
-        b_co(j).wait_send()
-
-    @pl.loop(0, NP)
-    def _(k):
-        for d in w_remote(k):
-            d.wait_send()
-        for i in range(6):
-            x_copy(k, i).wait_send()
-        for dz in (1, 2, 3):
-            z_copy(k, dz).wait_send()
-            za_copy(k, dz).wait_send()
-        for i in range(4):
-            xa_copy(k, i).wait_send()
-        for d in out_local(k):
-            d.wait()
-        for d in out_remote(k):
-            d.wait()
-
-    for i in (0, 1):
-        e1(i).wait_send()
+    for dy in (0, 1, 2, 3):
+        e1(dy).wait_send()
     for dy in (1, 2, 3):
         e2(dy).wait_send()
     e3().wait_send()
 
 
+def finish(*refs):
+    srcs, dsts, stage, ins, outs = refs[:5], refs[5:10], refs[10:15], refs[15], refs[16]
+    pairs = []
+    for a, b, m in zip(srcs, dsts, stage):
+        n = 4 if a.shape[0] > 64 else 1
+        step = a.shape[0] // n
+        for i in range(n):
+            part, k = pl.ds(i * step, step), len(pairs)
+            pairs.append(
+                (
+                    pltpu.make_async_copy(a.at[part], m.at[part], ins.at[k]),
+                    pltpu.make_async_copy(m.at[part], b.at[part], outs.at[k]),
+                )
+            )
+    for first, _ in pairs:
+        first.start()
+    for first, second in pairs:
+        first.wait()
+        second.start()
+    for _, second in pairs:
+        second.wait()
+
+
 def local(tokens, gate_weight, up_weight, down_weight, out_grad):
     def v(*shape, t=BF):
         return pltpu.VMEM(shape, t)
@@ -350,33 +463,43 @@
     def sem(*shape):
         return pltpu.SemaphoreType.DMA(shape) if shape else pltpu.SemaphoreType.DMA
 
-    W3 = 3 * W
     anywhere = pl.BlockSpec(memory_space=pl.ANY)
     vmem = pl.BlockSpec(memory_space=pltpu.VMEM)
     macs = 9 * 512 * 256 * 3584
-    return pl.pallas_call(
+    shapes = (
+        jax.ShapeDtypeStruct((64, 256), BF),
+        jax.ShapeDtypeStruct((64, 256), BF),
+        jax.ShapeDtypeStruct((256, 3584), BF),
+        jax.ShapeDtypeStruct((256, 3584), BF),
+        jax.ShapeDtypeStruct((3584, 256), BF),
+    )
+    results = pl.pallas_call(
         kernel,
-        out_shape=(
-            jax.ShapeDtypeStruct((64, 256), BF),
-            jax.ShapeDtypeStruct((64, 256), BF),
-            jax.ShapeDtypeStruct((256, 3584), BF),
-            jax.ShapeDtypeStruct((256, 3584), BF),
-            jax.ShapeDtypeStruct((3584, 256), BF),
-        ),
+        out_shape=shapes,
         in_specs=[anywhere] * 5,
         out_specs=(vmem, vmem, anywhere, anywhere, anywhere),
         scratch_shapes=[
             v(2, 512, 512),
             v(NP, 512, 2 * W),
             v(NP, W, 512),
-            v(4, 512, W3, t=F32),
-            v(NP, 512, W3),
-            v(NP, 2, 64, W3),
-            v(NP, 2, 64, W3),
-            v(NP, 2, 128, W3),
-            v(NP, 128, W3),
-            v(NP, 3, 32, W3),
-            v(NP, 512, W3),
+            v(5, 512, 2 * W, t=F32),
+            v(NP, 512, 2 * W),
+            v(NP, 2, 64, 2 * W),
+            v(NP, 2, 64, 2 * W),
+            v(NP, 2, 128, 2 * W),
+            v(NP, 128, 2 * W),
+            v(NP, 3, 32, 2 * W),
+            v(5, 4, 2, 2, 32, W, t=F32),
+            v(NP, 4, 2, 2, 32, W),
+            v(NP, 4, 2, 32, W),
+            v(NP, 4, 2, 32, W),
+            v(NP, 2, 32, W),
+            v(NP, 2, 32, W),
+            v(NP, 2, 2, 32, W),
+            v(NP, 32, W),
+            v(NP, 32, W),
+            v(NP, 512, 2 * W),
+            v(NP, 4, 2, 2, 32, W),
             v(NP, 512, 2 * W),
             v(NP, W, 512),
             v(2, 512, 512, t=F32),
@@ -389,8 +512,9 @@
             sem(), sem(), sem(2, 3), sem(2, 3), sem(8), sem(8),
             sem(NP, 6), sem(NP, 6), sem(NP, 3), sem(NP, 3),
             sem(NP, 3), sem(NP, 3), sem(NP, 4), sem(NP, 4),
+            sem(NP, 8), sem(NP, 8), sem(NP, 6), sem(NP, 6),
             sem(NP, 3), sem(NP, 3), sem(NP, 3),
-            sem(2), sem(2), sem(3), sem(3), sem(), sem(),
+            sem(4), sem(4), sem(3), sem(3), sem(), sem(),
         ],
         compiler_params=pltpu.CompilerParams(
             collective_id=0, has_side_effects=True, vmem_limit_bytes=60 * 2**20
@@ -398,6 +522,16 @@
         cost_estimate=pl.CostEstimate(flops=2 * macs, bytes_accessed=12 * 2**20, transcendentals=2**16),
         name="swiglu",
     )(tokens, gate_weight, up_weight, down_weight, out_grad)
+    return pl.pallas_call(
+        finish,
+        out_shape=shapes,
+        in_specs=[anywhere] * 5,
+        out_specs=(anywhere,) * 5,
+        scratch_shapes=[v(*a.shape) for a in shapes] + [sem(14), sem(14)],
+        compiler_params=pltpu.CompilerParams(vmem_limit_bytes=60 * 2**20),
+        cost_estimate=pl.CostEstimate(flops=0, bytes_accessed=12 * 2**20, transcendentals=0),
+        name="finish",
+    )(*results)
 
 
 def solution(mesh):

time: 146 us -> 129 us (0.88)
  local copies, waits for them, and re-layouts: 9.12 us -> 0 us
  Pallas kernels: 135 us -> 126 us
    unnamed x9 -> x0, local copies, waits for them, and re-layouts: 9.12 us -> none
    pallas_call x1 -> x2, Pallas kernels: 135 us -> 126 us  [the longest x1 121 us: local(): pl.pallas_call(kernel, out_shape=shapes, in_specs=[anywhere] * 5, out_spe...]
where the time goes in v2:
time: 129 us; the launch traced here: 127 us
  Pallas kernels  126 us (98%)
    pallas_call x1, Pallas kernels, local(): pl.pallas_call(kernel, out_shape=shapes, in_specs=[anywhere] * 5, out_spe...  121 us
    pallas_call x1, Pallas kernels, local(): pl.pallas_call(finish, out_shape=shapes, in_specs=[anywhere] * 5, out_spe...  5.1 us

profile of v2, /device:TPU:2, one launch (start us, length us, event | category | flops | bytes accessed | tf_op | source)
XLA Modules:
  0.0 127.1 jit_solution(6737679691753667167)
XLA Ops:
  0.6 121.4 %swiglu.1 = (bf16[64,256]{1,0:T(8,128)(2,1)}, bf16[64,256]{1,0:T(8,128)(2,1)}, bf16[256,3584]{1,0:T(8,128)(2,1)}, bf16[256,3584]{1,0:T(8,128)(2,1)}, bf16[3584,256]{1,0:T(8,128)(2,1)}) custom-call(bf16[64,256]{1,0:T(8,128)(2,1)} %tok.1, bf16[256,3584]{1,0:T(8,128)(2,1)} %gate_w.1, bf16[256,3584]{1,0:T(8,128)(2,1)} %up_w.1, bf16[3584,256]{1,0:T(8,128)(2,1)} %down_w.1, ...), custom_call_target="tpu_custom_call" | custom-call | flops 8455716864 | bytes 12582912 | tf_op jit(solution)/shard_map/swiglu/pallas_call | solution.py:476
  122.0 5.1 %finish.1 = (bf16[64,256]{1,0:T(8,128)(2,1)}, bf16[64,256]{1,0:T(8,128)(2,1)}, bf16[256,3584]{1,0:T(8,128)(2,1)}, bf16[256,3584]{1,0:T(8,128)(2,1)}, bf16[3584,256]{1,0:T(8,128)(2,1)}) custom-call(bf16[64,256]{1,0:T(8,128)(2,1)} %get-tuple-element.10.refs_0_, bf16[64,256]{1,0:T(8,128)(2,1)} %get-tuple-element.11.refs_1_, ...), custom_call_target="tpu_custom_call" | custom-call | bytes 12582912 | tf_op jit(solution)/shard_map/finish/pallas_call | solution.py:525

commit v3 on v2

v3 whole, which is shorter than its diff:
```python
import jax
import jax.numpy as jnp
from jax import lax
from jax.experimental import pallas as pl
from jax.experimental.pallas import tpu as pltpu
from jax.sharding import PartitionSpec as P

MESH = pl.DeviceIdType.MESH
BF = jnp.bfloat16
F32 = jnp.float32
NP = 7
W = 256
STARTS = (0, 1, 2, 3, 4, 5, 6)
AHEAD = 2
EARLY = 4
HALF = NP * W
F = 256


def dot(a, b, dims):
    return lax.dot_general(a, b, (dims, ((), ())), preferred_element_type=F32)


NN = ((1,), (0,))
NT = ((1,), (1,))
TN = ((0,), (0,))


def kernel(
    tok, gate_w, up_w, down_w, cot,
    lo_ref, tg_ref, gate_g, up_g, down_g,
    tc, wgu, wd, s32, sb, r1, a2, r2, yb, zr1, yc, zr2,
    h32, hs, hz1, hb, hr1, ha, hr2, hy, hz2, ag, hg, go, do, acc, e1b, e2b, e2r, e3b, e3r,
    in_l, wl, ws, wr, zh_s, zh_r, y_s, y_r, co_s, co_r,
    x_s, x_r, z_s, z_r, za_s, za_r, xa_s, xa_r, h_s, h_r, ha_s, ha_r, ol, os_, or_,
    e1_s, e1_r, e2_s, e2_r, e3_s, e3_r,
):
    row, col = lax.axis_index("row"), lax.axis_index("col")
    x, zl, c = row // 8, (row // 2) % 4, row % 2
    y, zh = col // 2, col % 2
    xp, xm, x2 = (x + 1) % 4, (x + 3) % 4, (x + 2) % 4

    def at_x(px):
        return (px * 8 + zl * 2 + c, col)

    def z_of(dz):
        b = (zl % 2) if dz % 2 == 0 else 1 - zl % 2
        h = (zl // 2) if dz < 2 else 1 - zl // 2
        return h * 2 + b

    def at_z(dz):
        return (x * 8 + z_of(dz) * 2 + c, col)

    def at_y(dy):
        return (row, ((y + dy) % 4) * 2 + zh)

    at_co = (x * 8 + zl * 2 + 1 - c, col)
    at_zh = (row, y * 2 + 1 - zh)
    peers = [at_co, at_zh, at_x(xp), at_x(xm)]
    peers += [at_z(d) for d in (1, 2)] + [at_y(d) for d in (1, 2, 3)]

    def remote(src, dst, ss, rs, dev):
        return pltpu.make_async_remote_copy(
            src_ref=src, dst_ref=dst, send_sem=ss, recv_sem=rs, device_id=dev, device_id_type=MESH
        )

    def cols(core, k):
        return pl.ds(pl.multiple_of(core * HALF + k * W, W), W)

    def feats(core):
        return pl.ds(pl.multiple_of(core * F, F), F)

    def rows(start, size):
        return pl.ds(pl.multiple_of(start, size), size)

    def w_local(k):
        return (
            pltpu.make_async_copy(gate_w.at[:, cols(c, k)], wgu.at[k, feats(c), pl.ds(0, W)], wl.at[k, 0]),
            pltpu.make_async_copy(up_w.at[:, cols(c, k)], wgu.at[k, feats(c), pl.ds(W, W)], wl.at[k, 1]),
            pltpu.make_async_copy(down_w.at[cols(c, k), :], wd.at[k, :, feats(c)], wl.at[k, 2]),
        )

    def w_remote(k):
        o = 1 - c
        return (
            remote(gate_w.at[:, cols(o, k)], wgu.at[k, feats(c), pl.ds(0, W)], ws.at[k, 0], wr.at[k, 0], at_co),
            remote(up_w.at[:, cols(o, k)], wgu.at[k, feats(c), pl.ds(W, W)], ws.at[k, 1], wr.at[k, 1], at_co),
            remote(down_w.at[cols(o, k), :], wd.at[k, :, feats(c)], ws.at[k, 2], wr.at[k, 2], at_co),
        )

    def block(j):
        return tc.at[:, j // 2, j % 2, :, feats(c)]

    def b_zh():
        return remote(block(col), block(col), zh_s, zh_r, at_zh)

    def b_y(h, dy):
        b = block(y * 2 + (zh if h == 0 else 1 - zh))
        return remote(b, b, y_s.at[h, dy - 1], y_r.at[h, dy - 1], at_y(dy))

    def b_co(j):
        return remote(block(j), block(j), co_s.at[j], co_r.at[j], at_co)

    ins = (
        pltpu.make_async_copy(tok, tc.at[0, y, zh, :, feats(c)], in_l.at[0]),
        pltpu.make_async_copy(cot, tc.at[1, y, zh, :, feats(c)], in_l.at[1]),
    )
    for d in ins:
        d.start()
    barrier = pltpu.get_barrier_semaphore()
    for p in peers:
        pl.semaphore_signal(barrier, inc=1, device_id=p, device_id_type=MESH)

    @pl.loop(0, NP)
    def _(k):
        for d in w_local(k):
            d.start()

    pl.semaphore_wait(barrier, len(peers))

    for d in ins:
        d.wait()
    b_zh().start()
    for dy in (1, 3, 2):
        b_y(0, dy).start()
    b_co(col).start()
    for k in range(AHEAD):
        for d in w_remote(k):
            d.start()

    b0, b1 = zl % 2, zl // 2

    def x_copy(k, i):
        if i == 0:
            src, dst, to = sb.at[k, x2, 0], r1.at[k, 0], xp
        elif i == 1:
            src, dst, to = sb.at[k, x2, 1], r1.at[k, 1], xm
        elif i == 2:
            src, dst, to = sb.at[k, xp, 1], r2.at[k, 0, 1], xp
        elif i == 3:
            src, dst, to = sb.at[k, xm, 0], r2.at[k, 1, 0], xm
        elif i == 4:
            src, dst, to = a2.at[k, 0], r2.at[k, 0, 0], xp
        else:
            src, dst, to = a2.at[k, 1], r2.at[k, 1, 1], xm
        return remote(src, dst, x_s.at[k, i], x_r.at[k, i], at_x(to))

    def z_copy(k, i):
        if i == 0:
            return remote(yb.at[k, :, 1 - b0], zr1.at[k], z_s.at[k, 0], z_r.at[k, 0], at_z(1))
        return remote(yc.at[k], zr2.at[k], z_s.at[k, 1], z_r.at[k, 1], at_z(2))

    def h_copy(k, i):
        to = xp if i in (1, 3, 5) else xm
        if i in (0, 8):
            src, dst = hs.at[k, :, i // 8, 1 - b0], hz1.at[k, :, i // 8]
        elif i == 1:
            src, dst = hb.at[k, x2, 0], hr1.at[k, 0]
        elif i == 2:
            src, dst = hb.at[k, x2, 1], hr1.at[k, 1]
        elif i == 3:
            src, dst = hb.at[k, xp, 1], hr2.at[k, 0, 1]
        elif i == 4:
            src, dst = hb.at[k, xm, 0], hr2.at[k, 1, 0]
        elif i == 5:
            src, dst = ha.at[k, 0], hr2.at[k, 0, 0]
        elif i == 6:
            src, dst = ha.at[k, 1], hr2.at[k, 1, 1]
        else:
            src, dst = hy.at[k], hz2.at[k]
        dev = at_z(1) if i in (0, 8) else at_z(2) if i == 7 else at_x(to)
        return remote(src, dst, h_s.at[k, i], h_r.at[k, i], dev)

    def za_copy(k, i):
        part, dev = (ag.at[k, x, b1, b0], at_z(2)) if i == 0 else (ag.at[k, x, :, b0], at_z(1))
        return remote(part, part, za_s.at[k, i], za_r.at[k, i], dev)

    def xa_copy(k, i):
        part = ag.at[k, x] if i < 2 else ag.at[k, xm, 0] if i == 2 else ag.at[k, xp, 1]
        return remote(part, part, xa_s.at[k, i], xa_r.at[k, i], at_x(xm if i % 2 else xp))

    def ha_copy(k, i):
        if i == 0:
            part, dev = hg.at[k, x, b1, b0], at_z(2)
        elif i == 1:
            part, dev = hg.at[k, x, :, b0], at_x(xp)
        elif i == 2:
            part, dev = hg.at[k, x, :, b0], at_x(xm)
        elif i == 3:
            part, dev = hg.at[k, xm, 0, b0], at_x(xp)
        elif i == 4:
            part, dev = hg.at[k, xp, 1, b0], at_x(xm)
        else:
            part, dev = hg.at[k, :, :, b0], at_z(1)
        return remote(part, part, ha_s.at[k, i], ha_r.at[k, i], dev)

    def out_refs(k, i, core):
        if i == 2:
            return do.at[k, :, feats(core)], down_g.at[cols(c, k), :]
        return go.at[k, feats(core), pl.ds(i * W, W)], (gate_g, up_g)[i].at[:, cols(c, k)]

    def out_local(k, i):
        return pltpu.make_async_copy(*out_refs(k, i, c), ol.at[k, i])

    def out_remote(k, i):
        return remote(*out_refs(k, i, 1 - c), os_.at[k, i], or_.at[k, i], at_co)

    def weights_here(k):
        for d in w_local(k):
            d.wait()
        for d in w_remote(k):
            d.wait_recv()

    def half(k, b):
        p = dot(tc[0, :, b].reshape(256, 512), wgu[k], NN).reshape(4, 64, 2 * W)
        s32[k, :, b] = p
        sb[k, :, b] = p.astype(BF)
        q = dot(tc[1, :, b].reshape(256, 512), wd[k], NT).reshape(4, 2, 32, W)
        h32[k, :, b] = q
        hs[k, :, b] = q.astype(BF)
        for which, sends in ((0, (0, 3, 0)), (1, (1, 2, 8))):

            @pl.when(b == which)
            def _(sends=sends):
                x_copy(k, sends[0]).start()
                x_copy(k, sends[1]).start()
                h_copy(k, sends[2]).start()

    def s0(k):
        @pl.when(k >= EARLY)
        def _():
            weights_here(k)
            half(k, zh)

        half(k, 1 - zh)

    def s1(k):
        x_copy(k, 0).wait_recv()
        a2[k, 0] = (s32[k, xp, 0] + r1[k, 0].astype(F32)).astype(BF)
        x_copy(k, 4).start()
        x_copy(k, 1).wait_recv()
        a2[k, 1] = (s32[k, xm, 1] + r1[k, 1].astype(F32)).astype(BF)
        x_copy(k, 5).start()
        h_copy(k, 0).wait_recv()
        h_copy(k, 8).wait_recv()
        half = h32[k, :, :, b0] + hz1[k].astype(F32)
        h32[k, :, :, b0] = half
        hb[k] = half.astype(BF)
        for i in (1, 2, 3, 4):
            h_copy(k, i).start()

    def s2(k):
        for i in (2, 3, 4, 5):
            x_copy(k, i).wait_recv()
        total = s32[k, x] + (r2[k, 0].astype(F32) + r2[k, 1].astype(F32))
        s32[k, x] = total
        yb[k] = total.astype(BF).reshape(2, 2, 32, 2 * W)
        z_copy(k, 0).start()
        h_copy(k, 1).wait_recv()
        ha[k, 0] = (h32[k, xp, 0, b0] + hr1[k, 0].astype(F32)).astype(BF)
        h_copy(k, 5).start()
        h_copy(k, 2).wait_recv()
        ha[k, 1] = (h32[k, xm, 1, b0] + hr1[k, 1].astype(F32)).astype(BF)
        h_copy(k, 6).start()

    def s3(k):
        z_copy(k, 0).wait_recv()
        mine = rows(b0 * 32, 32)
        yc[k] = (s32[k, x, 1 - b1, mine] + zr1[k, 1 - b1].astype(F32)).astype(BF)
        z_copy(k, 1).start()
        s32[k, x, b1, mine] = s32[k, x, b1, mine] + zr1[k, b1].astype(F32)
        for i in (3, 4, 5, 6):
            h_copy(k, i).wait_recv()
        total = h32[k, x, :, b0] + (hr2[k, 0].astype(F32) + hr2[k, 1].astype(F32))
        h32[k, x, :, b0] = total
        hy[k] = h32[k, x, 1 - b1, b0].astype(BF)
        h_copy(k, 7).start()

    def s4(k):
        z_copy(k, 1).wait_recv()
        total = s32[k, x, b1, rows(b0 * 32, 32)] + zr2[k].astype(F32)
        g, u = total[:, :W], total[:, W:]
        s = 1.0 / (1.0 + jnp.exp(-g))
        hg[k, x, b1, b0] = (g * s * u).astype(BF)
        ha_copy(k, 0).start()
        h_copy(k, 7).wait_recv()
        grad = h32[k, x, b1, b0] + hz2[k].astype(F32)
        ag[k, x, b1, b0, :, :W] = (grad * u * s * (1.0 + g * (1.0 - s))).astype(BF)
        ag[k, x, b1, b0, :, W:] = (grad * g * s).astype(BF)
        za_copy(k, 0).start()

    def s5(k):
        za_copy(k, 0).wait_recv()
        za_copy(k, 1).start()
        ha_copy(k, 0).wait_recv()
        ha_copy(k, 1).start()
        ha_copy(k, 2).start()

    def s6(k):
        za_copy(k, 1).wait_recv()
        xa_copy(k, 0).start()
        xa_copy(k, 1).start()
        ha_copy(k, 1).wait_recv()
        ha_copy(k, 3).start()
        ha_copy(k, 2).wait_recv()
        ha_copy(k, 4).start()

    def s7(k):
        xa_copy(k, 0).wait_recv()
        xa_copy(k, 2).start()
        xa_copy(k, 1).wait_recv()
        xa_copy(k, 3).start()
        ha_copy(k, 3).wait_recv()
        ha_copy(k, 4).wait_recv()
        ha_copy(k, 5).start()

    def deltas(k):
        return ag[k].reshape(512, 2 * W)

    def hidden(k):
        return hg[k].reshape(512, W)

    def add_token_grad(k):
        xa_copy(k, 2).wait_recv()
        xa_copy(k, 3).wait_recv()
        acc[1] += dot(deltas(k), wgu[k], NT)

    def add_layer_out(k):
        ha_copy(k, 5).wait_recv()
        acc[0] += dot(hidden(k), wd[k], NN)

    def weight_grads(k):
        go[k] = dot(tc[0].reshape(512, 512), deltas(k), TN).astype(BF)
        for i in range(2):
            out_remote(k, i).start()
            out_local(k, i).start()
        do[k] = dot(hidden(k), tc[1].reshape(512, 512), TN).astype(BF)
        out_remote(k, 2).start()
        out_local(k, 2).start()

    def s8(k):
        add_token_grad(k)
        add_layer_out(k)
        weight_grads(k)

    def forward(h):
        for dy in (1, 3, 2):
            b_y(h, dy).wait_recv()
            b_co(((y + 4 - dy) % 4) * 2 + (zh if h == 0 else 1 - zh)).start()

    def early(k):
        weights_here(k)
        half(k, zh)

    b_zh().wait_recv()
    for dy in (1, 2, 3):
        b_y(1, dy).start()
    forward(0)
    b_co(y * 2 + 1 - zh).start()

    @pl.loop(AHEAD, EARLY + 1)
    def _(k):
        for d in w_remote(k):
            d.start()

    acc[...] = jnp.zeros_like(acc)
    for p in range(4):
        b_co(p * 2 + zh).wait_recv()
    pl.loop(0, EARLY // 2)(early)
    forward(1)
    pl.loop(EARLY // 2, EARLY)(early)
    for p in range(4):
        b_co(p * 2 + 1 - zh).wait_recv()

    def begun(slot):
        return sum((slot + 63 - start) // 64 for start in STARTS)

    @pl.loop(0, STARTS[-1] + 9)
    def _(t):
        @pl.when(t < NP - EARLY - 1)
        def _():
            for d in w_remote(t + EARLY + 1):
                d.start()

        for lag, stage in ((0, s0), (2, s1), (3, s2), (4, s3), (5, s4), (6, s5), (7, s6), (8, s7), (9, s8)):

            @pl.loop(begun(t - lag), begun(t - lag + 1))
            def _(k, stage=stage):
                stage(k)

    def part(dy):
        return rows(((y + dy) % 4) * 128, 128)

    def e1(i, dy):
        src, dst = acc.at[i, part(dy), feats(1 - c)], e1b.at[i, part(dy)]
        return remote(src, dst, e1_s.at[i, dy], e1_r.at[i, dy], at_co)

    def e2(i, dy):
        src, n = e2b.at[i, part(dy)], dy - 1
        return remote(src, e2r.at[n, i], e2_s.at[i, n], e2_r.at[i, n], at_y(dy))

    def e3(i):
        return remote(e3b.at[i], e3r.at[i], e3_s.at[i], e3_r.at[i], at_zh)

    add_token_grad(NP - 1)
    for dy in (2, 1, 3, 0):
        e1(1, dy).start()
    add_layer_out(NP - 1)
    for dy in (2, 1, 3, 0):
        e1(0, dy).start()
    for i in (1, 0):
        for dy in (2, 1, 3):
            e1(i, dy).wait_recv()
            e2b[i, part(dy)] = (acc[i, part(dy), feats(c)] + e1b[i, part(dy)]).astype(BF)
            e2(i, dy).start()
    weight_grads(NP - 1)
    for i in (1, 0):
        e1(i, 0).wait_recv()
        e1b[i, part(0)] = acc[i, part(0), feats(c)] + e1b[i, part(0)]
    there, mine = rows(y * 128 + (1 - zh) * 64, 64), rows(y * 128 + zh * 64, 64)
    rt, rm = rows((1 - zh) * 64, 64), rows(zh * 64, 64)
    for i in (1, 0):
        for dy in (1, 3, 2):
            e2(i, dy).wait_recv()
        away = e1b[i, there]
        for n in range(3):
            away = away + e2r[n, i, rt].astype(F32)
        e3b[i] = away.astype(BF)
        e3(i).start()

    b_zh().wait_send()
    for h in (0, 1):
        for dy in (1, 2, 3):
            b_y(h, dy).wait_send()

    @pl.loop(0, 8)
    def _(j):
        b_co(j).wait_send()

    @pl.loop(0, NP)
    def _(k):
        for d in w_remote(k):
            d.wait_send()
        for i in range(6):
            x_copy(k, i).wait_send()
        for i in range(2):
            z_copy(k, i).wait_send()
            za_copy(k, i).wait_send()
        for i in range(4):
            xa_copy(k, i).wait_send()
        for i in range(9):
            h_copy(k, i).wait_send()
        for i in range(6):
            ha_copy(k, i).wait_send()
        for i in range(3):
            out_local(k, i).wait()
            out_remote(k, i).wait()

    for i, out in ((1, tg_ref), (0, lo_ref)):
        kept = e1b[i, mine]
        for n in range(3):
            kept = kept + e2r[n, i, rm].astype(F32)
        e3(i).wait_recv()
        out[...] = (kept + e3r[i].astype(F32)).astype(BF)

    for i in (0, 1):
        for dy in (0, 1, 2, 3):
            e1(i, dy).wait_send()
        for dy in (1, 2, 3):
            e2(i, dy).wait_send()
        e3(i).wait_send()


def finish(*refs):
    srcs, dsts, stage, ins, outs = refs[:5], refs[5:10], refs[10:15], refs[15], refs[16]
    pairs = []
    for a, b, m in zip(srcs, dsts, stage):
        n = 4 if a.shape[0] > 64 else 1
        step = a.shape[0] // n
        for i in range(n):
            part, k = pl.ds(i * step, step), len(pairs)
            pairs.append(
                (
                    pltpu.make_async_copy(a.at[part], m.at[part], ins.at[k]),
                    pltpu.make_async_copy(m.at[part], b.at[part], outs.at[k]),
                )
            )
    for first, _ in pairs:
        first.start()
    for first, second in pairs:
        first.wait()
        second.start()
    for _, second in pairs:
        second.wait()


def local(tokens, gate_weight, up_weight, down_weight, out_grad):
    def v(*shape, t=BF):
        return pltpu.VMEM(shape, t)

    def sem(*shape):
        return pltpu.SemaphoreType.DMA(shape) if shape else pltpu.SemaphoreType.DMA

    anywhere = pl.BlockSpec(memory_space=pl.ANY)
    vmem = pl.BlockSpec(memory_space=pltpu.VMEM)
    macs = 9 * 512 * 256 * 3584
    shapes = (
        jax.ShapeDtypeStruct((64, 256), BF),
        jax.ShapeDtypeStruct((64, 256), BF),
        jax.ShapeDtypeStruct((256, 3584), BF),
        jax.ShapeDtypeStruct((256, 3584), BF),
        jax.ShapeDtypeStruct((3584, 256), BF),
    )
    results = pl.pallas_call(
        kernel,
        out_shape=shapes,
        in_specs=[anywhere] * 5,
        out_specs=(vmem, vmem, anywhere, anywhere, anywhere),
        scratch_shapes=[
            v(2, 4, 2, 64, 512),
            v(NP, 512, 2 * W),
            v(NP, W, 512),
            v(NP, 4, 2, 64, 2 * W, t=F32),
            v(NP, 4, 2, 64, 2 * W),
            v(NP, 2, 64, 2 * W),
            v(NP, 2, 64, 2 * W),
            v(NP, 2, 2, 64, 2 * W),
            v(NP, 2, 2, 32, 2 * W),
            v(NP, 2, 32, 2 * W),
            v(NP, 32, 2 * W),
            v(NP, 32, 2 * W),
            v(NP, 4, 2, 2, 32, W, t=F32),
            v(NP, 4, 2, 2, 32, W),
            v(NP, 4, 2, 32, W),
            v(NP, 4, 2, 32, W),
            v(NP, 2, 32, W),
            v(NP, 2, 32, W),
            v(NP, 2, 2, 32, W),
            v(NP, 32, W),
            v(NP, 32, W),
            v(NP, 4, 2, 2, 32, 2 * W),
            v(NP, 4, 2, 2, 32, W),
            v(NP, 512, 2 * W),
            v(NP, W, 512),
            v(2, 512, 512, t=F32),
            v(2, 512, 256, t=F32),
            v(2, 512, 256),
            v(3, 2, 128, 256),
            v(2, 64, 256),
            v(2, 64, 256),
            sem(2), sem(NP, 3), sem(NP, 3), sem(NP, 3),
            sem(), sem(), sem(2, 3), sem(2, 3), sem(8), sem(8),
            sem(NP, 6), sem(NP, 6), sem(NP, 2), sem(NP, 2),
            sem(NP, 2), sem(NP, 2), sem(NP, 4), sem(NP, 4),
            sem(NP, 9), sem(NP, 9), sem(NP, 6), sem(NP, 6),
            sem(NP, 3), sem(NP, 3), sem(NP, 3),
            sem(2, 4), sem(2, 4), sem(2, 3), sem(2, 3), sem(2), sem(2),
        ],
        compiler_params=pltpu.CompilerParams(
            collective_id=0, has_side_effects=True, vmem_limit_bytes=60 * 2**20
        ),
        cost_estimate=pl.CostEstimate(flops=2 * macs, bytes_accessed=12 * 2**20, transcendentals=2**16),
        name="swiglu",
    )(tokens, gate_weight, up_weight, down_weight, out_grad)
    return pl.pallas_call(
        finish,
        out_shape=shapes,
        in_specs=[anywhere] * 5,
        out_specs=(anywhere,) * 5,
        scratch_shapes=[v(*a.shape) for a in shapes] + [sem(14), sem(14)],
        compiler_params=pltpu.CompilerParams(vmem_limit_bytes=60 * 2**20),
        cost_estimate=pl.CostEstimate(flops=0, bytes_accessed=12 * 2**20, transcendentals=0),
        name="finish",
    )(*results)


def solution(mesh):
    tokens, weights = P("col", "row"), P("row", "col")
    return jax.shard_map(
        local,
        mesh=mesh,
        in_specs=(tokens, weights, weights, tokens, tokens),
        out_specs=(tokens, tokens, weights, weights, tokens),
        check_vma=False,
    )
```

time: 129 us -> 123 us (0.953); the launches traced: 127 us -> 123 us
  Pallas kernels: 126 us -> 122 us
    pallas_call x1, Pallas kernels: 121 us -> 117 us  [local(): pl.pallas_call(kernel, out_shape=shapes, in_specs=[anywhere] * 5, out_spe...]
where the time goes in v3:
time: 123 us
  Pallas kernels  122 us (99%)
    pallas_call x1, Pallas kernels, local(): pl.pallas_call(kernel, out_shape=shapes, in_specs=[anywhere] * 5, out_spe...  117 us
    pallas_call x1, Pallas kernels, local(): pl.pallas_call(finish, out_shape=shapes, in_specs=[anywhere] * 5, out_spe...  5.1 us

profile of v3, /device:TPU:2, one launch (start us, length us, event | category | flops | bytes accessed | tf_op | source)
XLA Modules:
  0.0 122.9 jit_solution(5783198786562294254)
XLA Ops:
  0.6 117.1 %swiglu.1 = (bf16[64,256]{1,0:T(8,128)(2,1)}, bf16[64,256]{1,0:T(8,128)(2,1)}, bf16[256,3584]{1,0:T(8,128)(2,1)}, bf16[256,3584]{1,0:T(8,128)(2,1)}, bf16[3584,256]{1,0:T(8,128)(2,1)}) custom-call(bf16[64,256]{1,0:T(8,128)(2,1)} %tok.1, bf16[256,3584]{1,0:T(8,128)(2,1)} %gate_w.1, bf16[256,3584]{1,0:T(8,128)(2,1)} %up_w.1, bf16[3584,256]{1,0:T(8,128)(2,1)} %down_w.1, ...), custom_call_target="tpu_custom_call" | custom-call | flops 8455716864 | bytes 12582912 | tf_op jit(solution)/shard_map/swiglu/pallas_call | solution.py:514
  117.8 5.1 %finish.1 = (bf16[64,256]{1,0:T(8,128)(2,1)}, bf16[64,256]{1,0:T(8,128)(2,1)}, bf16[256,3584]{1,0:T(8,128)(2,1)}, bf16[256,3584]{1,0:T(8,128)(2,1)}, bf16[3584,256]{1,0:T(8,128)(2,1)}) custom-call(bf16[64,256]{1,0:T(8,128)(2,1)} %get-tuple-element.10.refs_0_, bf16[64,256]{1,0:T(8,128)(2,1)} %get-tuple-element.11.refs_1_, ...), custom_call_target="tpu_custom_call" | custom-call | bytes 12582912 | tf_op jit(solution)/shard_map/finish/pallas_call | solution.py:565

commit v4 on v3

--- a/solution.py
+++ b/solution.py
@@ -10,7 +10,6 @@
 F32 = jnp.float32
 NP = 7
 W = 256
-STARTS = (0, 1, 2, 3, 4, 5, 6)
 AHEAD = 2
 EARLY = 4
 HALF = NP * W
@@ -57,7 +56,7 @@
     at_co = (x * 8 + zl * 2 + 1 - c, col)
     at_zh = (row, y * 2 + 1 - zh)
     peers = [at_co, at_zh, at_x(xp), at_x(xm)]
-    peers += [at_z(d) for d in (1, 2)] + [at_y(d) for d in (1, 2, 3)]
+    peers += [at_z(d) for d in (1, 2, 3)] + [at_y(d) for d in (1, 2, 3)]
 
     def remote(src, dst, ss, rs, dev):
         return pltpu.make_async_remote_copy(
@@ -171,9 +170,9 @@
         dev = at_z(1) if i in (0, 8) else at_z(2) if i == 7 else at_x(to)
         return remote(src, dst, h_s.at[k, i], h_r.at[k, i], dev)
 
-    def za_copy(k, i):
-        part, dev = (ag.at[k, x, b1, b0], at_z(2)) if i == 0 else (ag.at[k, x, :, b0], at_z(1))
-        return remote(part, part, za_s.at[k, i], za_r.at[k, i], dev)
+    def za_copy(k, dz):
+        part = ag.at[k, x, b1, b0]
+        return remote(part, part, za_s.at[k, dz - 1], za_r.at[k, dz - 1], at_z(dz))
 
     def xa_copy(k, i):
         part = ag.at[k, x] if i < 2 else ag.at[k, xm, 0] if i == 2 else ag.at[k, xp, 1]
@@ -287,32 +286,33 @@
         grad = h32[k, x, b1, b0] + hz2[k].astype(F32)
         ag[k, x, b1, b0, :, :W] = (grad * u * s * (1.0 + g * (1.0 - s))).astype(BF)
         ag[k, x, b1, b0, :, W:] = (grad * g * s).astype(BF)
-        za_copy(k, 0).start()
+        for dz in (2, 1, 3):
+            za_copy(k, dz).start()
 
     def s5(k):
-        za_copy(k, 0).wait_recv()
-        za_copy(k, 1).start()
         ha_copy(k, 0).wait_recv()
         ha_copy(k, 1).start()
         ha_copy(k, 2).start()
-
-    def s6(k):
-        za_copy(k, 1).wait_recv()
+        for dz in (1, 2, 3):
+            za_copy(k, dz).wait_recv()
         xa_copy(k, 0).start()
         xa_copy(k, 1).start()
+
+    def s6(k):
         ha_copy(k, 1).wait_recv()
         ha_copy(k, 3).start()
         ha_copy(k, 2).wait_recv()
         ha_copy(k, 4).start()
-
-    def s7(k):
         xa_copy(k, 0).wait_recv()
         xa_copy(k, 2).start()
         xa_copy(k, 1).wait_recv()
         xa_copy(k, 3).start()
+
+    def s7(k):
         ha_copy(k, 3).wait_recv()
         ha_copy(k, 4).wait_recv()
         ha_copy(k, 5).start()
+        add_token_grad(k)
 
     def deltas(k):
         return ag[k].reshape(512, 2 * W)
@@ -339,7 +339,6 @@
         out_local(k, 2).start()
 
     def s8(k):
-        add_token_grad(k)
         add_layer_out(k)
         weight_grads(k)
 
@@ -372,10 +371,7 @@
     for p in range(4):
         b_co(p * 2 + 1 - zh).wait_recv()
 
-    def begun(slot):
-        return sum((slot + 63 - start) // 64 for start in STARTS)
-
-    @pl.loop(0, STARTS[-1] + 9)
+    @pl.loop(0, NP + 8)
     def _(t):
         @pl.when(t < NP - EARLY - 1)
         def _():
@@ -383,9 +379,10 @@
                 d.start()
 
         for lag, stage in ((0, s0), (2, s1), (3, s2), (4, s3), (5, s4), (6, s5), (7, s6), (8, s7), (9, s8)):
-
-            @pl.loop(begun(t - lag), begun(t - lag + 1))
-            def _(k, stage=stage):
+            k = t - lag
+
+            @pl.when((k >= 0) & (k < NP - (stage is s8)))
+            def _(k=k, stage=stage):
                 stage(k)
 
     def part(dy):
@@ -402,17 +399,19 @@
     def e3(i):
         return remote(e3b.at[i], e3r.at[i], e3_s.at[i], e3_r.at[i], at_zh)
 
-    add_token_grad(NP - 1)
-    for dy in (2, 1, 3, 0):
-        e1(1, dy).start()
-    add_layer_out(NP - 1)
-    for dy in (2, 1, 3, 0):
-        e1(0, dy).start()
-    for i in (1, 0):
+    def over_cores(i):
         for dy in (2, 1, 3):
             e1(i, dy).wait_recv()
             e2b[i, part(dy)] = (acc[i, part(dy), feats(c)] + e1b[i, part(dy)]).astype(BF)
             e2(i, dy).start()
+
+    for dy in (2, 1, 3, 0):
+        e1(1, dy).start()
+    over_cores(1)
+    add_layer_out(NP - 1)
+    for dy in (2, 1, 3, 0):
+        e1(0, dy).start()
+    over_cores(0)
     weight_grads(NP - 1)
     for i in (1, 0):
         e1(i, 0).wait_recv()
@@ -445,7 +444,8 @@
             x_copy(k, i).wait_send()
         for i in range(2):
             z_copy(k, i).wait_send()
-            za_copy(k, i).wait_send()
+        for dz in (1, 2, 3):
+            za_copy(k, dz).wait_send()
         for i in range(4):
             xa_copy(k, i).wait_send()
         for i in range(9):
@@ -551,7 +551,7 @@
             sem(2), sem(NP, 3), sem(NP, 3), sem(NP, 3),
             sem(), sem(), sem(2, 3), sem(2, 3), sem(8), sem(8),
             sem(NP, 6), sem(NP, 6), sem(NP, 2), sem(NP, 2),
-            sem(NP, 2), sem(NP, 2), sem(NP, 4), sem(NP, 4),
+            sem(NP, 3), sem(NP, 3), sem(NP, 4), sem(NP, 4),
             sem(NP, 9), sem(NP, 9), sem(NP, 6), sem(NP, 6),
             sem(NP, 3), sem(NP, 3), sem(NP, 3),
             sem(2, 4), sem(2, 4), sem(2, 3), sem(2, 3), sem(2), sem(2),

time: 123 us -> 123 us (level)
  no operation moved by 1% of the time
where the time goes in v4:
time: 123 us; the launch traced here: 122 us
  Pallas kernels  121 us (98%)
    pallas_call x1, Pallas kernels, local(): pl.pallas_call(kernel, out_shape=shapes, in_specs=[anywhere] * 5, out_spe...  116 us
    pallas_call x1, Pallas kernels, local(): pl.pallas_call(finish, out_shape=shapes, in_specs=[anywhere] * 5, out_spe...  5.1 us

profile of v4, /device:TPU:2, one launch (start us, length us, event | category | flops | bytes accessed | tf_op | source)
XLA Modules:
  0.0 121.8 jit_solution(18047616456895118435)
XLA Ops:
  0.6 116.1 %swiglu.1 = (bf16[64,256]{1,0:T(8,128)(2,1)}, bf16[64,256]{1,0:T(8,128)(2,1)}, bf16[256,3584]{1,0:T(8,128)(2,1)}, bf16[256,3584]{1,0:T(8,128)(2,1)}, bf16[3584,256]{1,0:T(8,128)(2,1)}) custom-call(bf16[64,256]{1,0:T(8,128)(2,1)} %tok.1, bf16[256,3584]{1,0:T(8,128)(2,1)} %gate_w.1, bf16[256,3584]{1,0:T(8,128)(2,1)} %up_w.1, bf16[3584,256]{1,0:T(8,128)(2,1)} %down_w.1, ...), custom_call_target="tpu_custom_call" | custom-call | flops 8455716864 | bytes 12582912 | tf_op jit(solution)/shard_map/swiglu/pallas_call | solution.py:514
  116.7 5.1 %finish.1 = (bf16[64,256]{1,0:T(8,128)(2,1)}, bf16[64,256]{1,0:T(8,128)(2,1)}, bf16[256,3584]{1,0:T(8,128)(2,1)}, bf16[256,3584]{1,0:T(8,128)(2,1)}, bf16[3584,256]{1,0:T(8,128)(2,1)}) custom-call(bf16[64,256]{1,0:T(8,128)(2,1)} %get-tuple-element.10.refs_0_, bf16[64,256]{1,0:T(8,128)(2,1)} %get-tuple-element.11.refs_1_, ...), custom_call_target="tpu_custom_call" | custom-call | bytes 12582912 | tf_op jit(solution)/shard_map/finish/pallas_call | solution.py:565

commit v5 on v4

--- a/solution.py
+++ b/solution.py
@@ -10,7 +10,7 @@
 F32 = jnp.float32
 NP = 7
 W = 256
-AHEAD = 2
+AHEAD = 1
 EARLY = 4
 HALF = NP * W
 F = 256

time: 123 us -> 123 us (level)
  no operation moved by 1% of the time
where the time goes in v5:
time: 123 us; the launch traced here: 122 us
  Pallas kernels  121 us (98%)
    pallas_call x1, Pallas kernels, local(): pl.pallas_call(kernel, out_shape=shapes, in_specs=[anywhere] * 5, out_spe...  116 us
    pallas_call x1, Pallas kernels, local(): pl.pallas_call(finish, out_shape=shapes, in_specs=[anywhere] * 5, out_spe...  5.1 us

profile of v5, /device:TPU:2, one launch (start us, length us, event | category | flops | bytes accessed | tf_op | source)
XLA Modules:
  0.0 121.7 jit_solution(7417024359925648078)
XLA Ops:
  0.6 115.9 %swiglu.1 = (bf16[64,256]{1,0:T(8,128)(2,1)}, bf16[64,256]{1,0:T(8,128)(2,1)}, bf16[256,3584]{1,0:T(8,128)(2,1)}, bf16[256,3584]{1,0:T(8,128)(2,1)}, bf16[3584,256]{1,0:T(8,128)(2,1)}) custom-call(bf16[64,256]{1,0:T(8,128)(2,1)} %tok.1, bf16[256,3584]{1,0:T(8,128)(2,1)} %gate_w.1, bf16[256,3584]{1,0:T(8,128)(2,1)} %up_w.1, bf16[3584,256]{1,0:T(8,128)(2,1)} %down_w.1, ...), custom_call_target="tpu_custom_call" | custom-call | flops 8455716864 | bytes 12582912 | tf_op jit(solution)/shard_map/swiglu/pallas_call | solution.py:514
  116.6 5.1 %finish.1 = (bf16[64,256]{1,0:T(8,128)(2,1)}, bf16[64,256]{1,0:T(8,128)(2,1)}, bf16[256,3584]{1,0:T(8,128)(2,1)}, bf16[256,3584]{1,0:T(8,128)(2,1)}, bf16[3584,256]{1,0:T(8,128)(2,1)}) custom-call(bf16[64,256]{1,0:T(8,128)(2,1)} %get-tuple-element.10.refs_0_, bf16[64,256]{1,0:T(8,128)(2,1)} %get-tuple-element.11.refs_1_, ...), custom_call_target="tpu_custom_call" | custom-call | bytes 12582912 | tf_op jit(solution)/shard_map/finish/pallas_call | solution.py:565
